TPU v7x, 128 devices: a whole 4x4x4 slice. The times are simulated.
128 devices in a mesh: dp: 16 (over y, z_hi, core), row: 4 (over x), col: 2 (over z_lo).
Axes of the slice: x: 4, y: 4, z: 4 (z_hi: 2, z_lo: 2; z = z_hi * 2 + z_lo), core: 2. Of those that a mesh axis runs over, the one named last changes fastest.
Arguments:
- inputs: bfloat16 [16, 1024, 1152], P('dp', 'row', 'col'), may hold values from -6 to 6
- w_query: bfloat16 [1152, 1024], P('col', 'row'), may hold values from -0.1875 to 0.1875
- w_key: bfloat16 [1152, 256], P('col'), may hold values from -0.1875 to 0.1875
- w_value: bfloat16 [1152, 256], P('col'), may hold values from -0.1875 to 0.1875
- attention_output_weight: bfloat16 [1024, 1152], P('row', 'col'), may hold values from -0.1875 to 0.1875
- w_gate: bfloat16 [1152, 6912], P('col', 'row'), may hold values from -0.1875 to 0.1875
- w_up: bfloat16 [1152, 6912], P('col', 'row'), may hold values from -0.1875 to 0.1875
- down_weight: bfloat16 [6912, 1152], P('row', 'col'), may hold values from -0.078125 to 0.078125
- g_in: float32 [1152], P('col'), may hold values from 0.25 to 1.75
- g_query: float32 [256], replicated, may hold values from 0.25 to 1.75
- g_key: float32 [256], replicated, may hold values from 0.25 to 1.75
- g_post_attn: float32 [1152], P('col'), may hold values from 0.25 to 1.75
- g_pre_ffn: float32 [1152], P('col'), may hold values from 0.25 to 1.75
- g_post_ffn: float32 [1152], P('col'), may hold values from 0.25 to 1.75
- cotangent: bfloat16 [16, 1024, 1152], P('dp', 'row', 'col'), may hold values from -6 to 6
Outputs:
- block_out: bfloat16 [16, 1024, 1152], P('dp', 'row', 'col')
- grad_inputs: bfloat16 [16, 1024, 1152], P('dp', 'row', 'col')
- grad_w_query: float32 [1152, 1024], P('col', 'row')
- grad_w_key: float32 [1152, 256], P('col')
- grad_w_value: float32 [1152, 256], P('col')
- grad_w_out: float32 [1024, 1152], P('row', 'col')
- grad_w_gate: float32 [1152, 6912], P('col', 'row')
- grad_w_up: float32 [1152, 6912], P('col', 'row')
- grad_w_down: float32 [6912, 1152], P('row', 'col')
- grad_g_in: float32 [1152], P('col')
- grad_g_query: float32 [256], replicated
- grad_g_key: float32 [256], replicated
- grad_g_post_attn: float32 [1152], P('col')
- grad_g_pre_ffn: float32 [1152], P('col')
- grad_g_post_ffn: float32 [1152], P('col')
All inputs are finite; a program needn't handle non-finite values.
Results may differ from a plain program's by a relative error of at most 0.025.
Values may be sent and summed in bfloat16 or wider, within the bound.
No kernel may reach another device: no remote copies, remote signals or barrier semaphores. Data moves between devices by JAX's collectives and lax.ppermute only.
A program may use at most 128 MiB of HBM per device.

v0:
```python
from functools import partial

import jax
import jax.numpy as jnp
from jax import lax
from jax.sharding import PartitionSpec as P

WINDOW = 512


EPSILON = 1e-06
MASKED = -1e30
ROPE_BASE = 10000.0


def sent_to_all(shard, axis):
    copies = jnp.broadcast_to(shard, (lax.axis_size(axis), *shard.shape))
    return lax.all_to_all(copies, axis, split_axis=0, concat_axis=0, tiled=True)


def of_everyone(shard, axis):
    return sent_to_all(shard, axis).sum(axis=0)


def laid_out(parts, dim):
    shape = list(parts.shape[1:])
    shape[dim] *= parts.shape[0]
    return jnp.moveaxis(parts, 0, dim).reshape(shape)


def gather_directly(shard, axis, dim):
    return laid_out(sent_to_all(shard, axis), dim)


def cut_along(shard, dim, length):
    before, after = (shard.shape[:dim], shard.shape[dim + 1 :])
    return jnp.moveaxis(shard.reshape(*before, length, -1, *after), dim, 0)


def summed_on_arrival(shard, axis, dim):
    length = lax.axis_size(axis)
    parts = lax.all_to_all(cut_along(shard, dim, length), axis, 0, 0, tiled=True)
    return jnp.sum(parts.astype(jnp.float32), axis=0)


def passed_along(block, axis, distance):
    devices = range(lax.axis_size(axis))
    route = [(i - distance, i) for i in devices if i - distance in devices]
    return lax.ppermute(block, axis, route)


def feature_sums(partial_sum):
    return of_everyone(partial_sum, "col")


def row_gather(values):
    return gather_directly(values, "row", 1)


def col_gather(values):
    return lax.all_gather(values, "col", axis=1, tiled=True)


def row_sums(values):
    return summed_on_arrival(values.astype(jnp.bfloat16), "row", 1)


def reduce_feature_axis(full_rows, weight_whole, pattern):
    whole_rows = lax.all_to_all(full_rows, "col", split_axis=1, concat_axis=2, tiled=True)
    return jnp.einsum(pattern, whole_rows, weight_whole, preferred_element_type=jnp.float32)


def norm_forward(values, gain_vec, feature_count):
    squares = feature_sums(jnp.sum(values * values, axis=-1, keepdims=True))
    factor = lax.rsqrt(squares / feature_count + EPSILON)
    return (values * factor * gain_vec, factor)


def norm_backward(values, factor, gain_vec, upstream, feature_count):
    scaled = upstream * gain_vec
    inner = feature_sums(jnp.sum(scaled * values, axis=-1, keepdims=True))
    grad_values = factor * scaled - values * (factor * factor * factor) * inner / feature_count
    grad_gain = jnp.sum(upstream * values * factor, axis=(0, 1))
    return (grad_values, grad_gain)


def rotate(values, position):
    half_size = values.shape[-1] // 2
    exponent = jnp.arange(half_size, dtype=jnp.float32) * (2.0 / values.shape[-1])
    angles = position.astype(jnp.float32)[:, None] * (ROPE_BASE ** (-exponent))[None, :]
    cosine = jnp.cos(angles)
    sine = jnp.sin(angles)
    first = values[..., :half_size]
    second = values[..., half_size:]
    return jnp.concatenate(
        [first * cosine - second * sine, second * cosine + first * sine], axis=-1
    )


def head_map(raw_heads, gain_vec, position, scaling):
    normed = (
        raw_heads
        * lax.rsqrt(jnp.mean(raw_heads * raw_heads, axis=-1, keepdims=True) + EPSILON)
        * gain_vec
    )
    return rotate(normed, position) * scaling


def geglu(gate_proj, up_proj):
    return jax.nn.gelu(gate_proj, approximate=True) * up_proj


def local(
    inputs,
    w_query,
    w_key,
    w_value,
    attention_output_weight,
    w_gate,
    w_up,
    down_weight,
    g_in,
    g_query,
    g_key,
    g_post_attn,
    g_pre_ffn,
    g_post_ffn,
    cotangent,
):
    col_count = lax.axis_size("col")
    col_index = lax.axis_index("col")
    seq_count, row_share, feature_share = inputs.shape
    feature_count = feature_share * col_count
    head_size = g_query.shape[0]
    heads_local = w_query.shape[1] // head_size
    query_width = heads_local * head_size
    hidden_share = w_gate.shape[1]
    length = row_share * lax.axis_size("row")
    half_rows = length // col_count
    position = col_index * half_rows + jnp.arange(half_rows, dtype=jnp.int32)
    key_position = (col_index - 1) * half_rows + jnp.arange(2 * half_rows, dtype=jnp.int32)
    offset = position[:, None] - key_position[None, :]
    allowed = (offset >= 0) & (offset < WINDOW) & (key_position[None, :] >= 0)
    query_key_value_weight = jnp.concatenate([w_query, w_key, w_value], axis=1)
    paired_weight = jnp.concatenate([w_gate, w_up], axis=1)
    qkv_whole, pair_whole, out_whole, down_whole = (
        lax.all_gather(query_key_value_weight, "col", axis=0, tiled=True),
        lax.all_gather(paired_weight, "col", axis=0, tiled=True),
        lax.all_gather(attention_output_weight, "col", axis=1, tiled=True),
        lax.all_gather(down_weight, "col", axis=1, tiled=True),
    )
    inputs_wide = inputs.astype(jnp.float32)
    attn_norm, attn_factor = norm_forward(inputs_wide, g_in, feature_count)
    attention_complete = row_gather(attn_norm.astype(jnp.bfloat16))
    query_key_value_total = reduce_feature_axis(attention_complete, qkv_whole, "rit,th->rih")
    raw_query = (
        query_key_value_total[..., :query_width]
        .reshape(seq_count, half_rows, heads_local, head_size)
        .transpose(0, 2, 1, 3)
    )
    raw_key = query_key_value_total[:, None, :, query_width : query_width + head_size]
    value_low = query_key_value_total[..., query_width + head_size :].astype(jnp.bfloat16)
    query_rot, query_pull = jax.vjp(
        partial(head_map, position=position, scaling=head_size ** (-0.5)), raw_query, g_query
    )
    key_rot, key_pull = jax.vjp(partial(head_map, position=position, scaling=1.0), raw_key, g_key)
    query_low = query_rot.astype(jnp.bfloat16)
    key_low = key_rot[:, 0].astype(jnp.bfloat16)
    key_prev, value_prev = passed_along((key_low, value_low), "col", 1)
    key_all = jnp.concatenate([key_prev, key_low], axis=1)
    value_all = jnp.concatenate([value_prev, value_low], axis=1)
    scores = jnp.where(
        allowed,
        jnp.einsum("shqd,skd->shqk", query_low, key_all, preferred_element_type=jnp.float32),
        MASKED,
    )
    largest = jnp.max(scores, axis=-1, keepdims=True)
    summed = jnp.sum(jnp.exp(scores - largest), axis=-1, keepdims=True)
    log_total = largest + jnp.log(summed)
    attn_probs = jnp.exp(scores - log_total)
    mixed_heads = jnp.einsum(
        "shqk,skd->shqd",
        attn_probs.astype(jnp.bfloat16),
        value_all,
        preferred_element_type=jnp.float32,
    )
    mixed_low = (
        mixed_heads.astype(jnp.bfloat16)
        .transpose(0, 2, 1, 3)
        .reshape(seq_count, half_rows, query_width)
    )
    mixed_complete = col_gather(mixed_low)
    branch = row_sums(
        jnp.einsum(
            "cfb,bi->cfi",
            mixed_complete,
            attention_output_weight,
            preferred_element_type=jnp.float32,
        )
    )
    post_attn, post_factor = norm_forward(branch, g_post_attn, feature_count)
    middle = inputs_wide + post_attn
    ffn_norm, ffn_factor = norm_forward(middle, g_pre_ffn, feature_count)
    feedforward_complete = row_gather(ffn_norm.astype(jnp.bfloat16))
    paired_partial_total = reduce_feature_axis(feedforward_complete, pair_whole, "nax,xu->nau")
    hidden, geglu_pull = jax.vjp(
        geglu, paired_partial_total[..., :hidden_share], paired_partial_total[..., hidden_share:]
    )
    hidden_complete = col_gather(hidden.astype(jnp.bfloat16))
    down_proj = row_sums(
        jnp.einsum("yat,tn->yan", hidden_complete, down_weight, preferred_element_type=jnp.float32)
    )
    post_ffn, post_ffn_factor = norm_forward(down_proj, g_post_ffn, feature_count)
    block_out = (middle + post_ffn).astype(jnp.bfloat16)
    upstream = cotangent.astype(jnp.float32)
    grad_down, grad_g_post_ffn = norm_backward(
        down_proj, post_ffn_factor, g_post_ffn, upstream, feature_count
    )
    down_gradient_complete = row_gather(grad_down.astype(jnp.bfloat16))
    grad_w_down = jnp.einsum(
        "hwk,hwj->kj", hidden_complete, down_gradient_complete, preferred_element_type=jnp.float32
    )
    hidden_gradient = reduce_feature_axis(down_gradient_complete, down_whole, "qrn,on->qro")
    grad_gate, grad_up = geglu_pull(hidden_gradient)
    grad_pair = jnp.concatenate(
        [grad_gate.astype(jnp.bfloat16), grad_up.astype(jnp.bfloat16)], axis=-1
    )
    paired_gradient_complete = col_gather(grad_pair)
    grad_w_pair = jnp.einsum(
        "wkb,wkg->bg",
        feedforward_complete,
        paired_gradient_complete,
        preferred_element_type=jnp.float32,
    )
    grad_w_gate = grad_w_pair[:, :hidden_share]
    grad_w_up = grad_w_pair[:, hidden_share:]
    grad_ffn_in = row_sums(
        jnp.einsum(
            "bvq,eq->bve",
            paired_gradient_complete,
            paired_weight,
            preferred_element_type=jnp.float32,
        )
    )
    grad_mid_norm, grad_g_pre_ffn = norm_backward(
        middle, ffn_factor, g_pre_ffn, grad_ffn_in, feature_count
    )
    grad_middle = upstream + grad_mid_norm
    grad_branch, grad_g_post_attn = norm_backward(
        branch, post_factor, g_post_attn, grad_middle, feature_count
    )
    branch_gradient_complete = row_gather(grad_branch.astype(jnp.bfloat16))
    grad_w_out = jnp.einsum(
        "jyh,jyp->hp", mixed_complete, branch_gradient_complete, preferred_element_type=jnp.float32
    )
    mixed_gradient = reduce_feature_axis(branch_gradient_complete, out_whole, "afm,rm->afr")
    grad_mixed_low = (
        mixed_gradient.astype(jnp.bfloat16)
        .reshape(seq_count, half_rows, heads_local, head_size)
        .transpose(0, 2, 1, 3)
    )
    scores_again = jnp.where(
        allowed,
        jnp.einsum("shqd,skd->shqk", query_low, key_all, preferred_element_type=jnp.float32),
        MASKED,
    )
    probs_again = jnp.exp(scores_again - log_total)
    grad_probs = jnp.einsum(
        "shqd,skd->shqk", grad_mixed_low, value_all, preferred_element_type=jnp.float32
    )
    grad_value_all = jnp.einsum(
        "shqk,shqd->shkd",
        probs_again.astype(jnp.bfloat16),
        grad_mixed_low,
        preferred_element_type=jnp.float32,
    )
    grad_scores = (
        probs_again * (grad_probs - jnp.sum(probs_again * grad_probs, axis=-1, keepdims=True))
    ).astype(jnp.bfloat16)
    grad_query_rot = jnp.einsum(
        "shqk,skd->shqd", grad_scores, key_all, preferred_element_type=jnp.float32
    )
    grad_key_all = jnp.einsum(
        "shqk,shqd->shkd", grad_scores, query_low, preferred_element_type=jnp.float32
    )
    key_back, value_back = (
        passed_along(grad_key_all[:, :, :half_rows].astype(jnp.bfloat16), "col", -1).astype(
            jnp.float32
        ),
        passed_along(grad_value_all[:, :, :half_rows].astype(jnp.bfloat16), "col", -1).astype(
            jnp.float32
        ),
    )
    grad_key_rot = grad_key_all[:, :, half_rows:] + key_back
    grad_value_heads = grad_value_all[:, :, half_rows:] + value_back
    grad_query_heads, grad_g_query = query_pull(grad_query_rot)
    grad_key_heads, grad_g_key = key_pull(grad_key_rot)

    def heads_last(values):
        return (
            values.astype(jnp.bfloat16)
            .transpose(0, 2, 1, 3)
            .reshape(seq_count, half_rows, query_width)
        )

    grad_qkv = jnp.concatenate(
        [heads_last(grad_query_heads), heads_last(grad_key_heads), heads_last(grad_value_heads)],
        axis=-1,
    )
    query_key_value_gradient = col_gather(grad_qkv)
    reverse_weight = jnp.concatenate(
        [w_query, jnp.tile(w_key, (1, heads_local)), jnp.tile(w_value, (1, heads_local))], axis=1
    )
    grad_w_back = jnp.einsum(
        "pfi,pfj->ij",
        attention_complete,
        query_key_value_gradient,
        preferred_element_type=jnp.float32,
    )
    grad_w_query = grad_w_back[:, :query_width]
    grad_w_key = (
        grad_w_back[:, query_width : 2 * query_width]
        .reshape(feature_share, heads_local, head_size)
        .sum(axis=1)
    )
    grad_w_value = (
        grad_w_back[:, 2 * query_width :].reshape(feature_share, heads_local, head_size).sum(axis=1)
    )
    grad_attn_in = row_sums(
        jnp.einsum(
            "fpy,ty->fpt",
            query_key_value_gradient,
            reverse_weight,
            preferred_element_type=jnp.float32,
        )
    )
    grad_in_norm, grad_g_in = norm_backward(
        inputs_wide, attn_factor, g_in, grad_attn_in, feature_count
    )
    grad_inputs = (grad_middle + grad_in_norm).astype(jnp.bfloat16)
    grad_head_gains = feature_sums(jnp.concatenate([grad_g_query, grad_g_key]))
    shared = lax.psum(
        (
            grad_w_key,
            grad_w_value,
            grad_g_in,
            grad_g_post_attn,
            grad_g_pre_ffn,
            grad_g_post_ffn,
            grad_head_gains,
        ),
        ("dp", "row"),
    )
    grad_w_query, grad_w_out, grad_w_gate, grad_w_up, grad_w_down = (
        lax.psum(grad_w_query.astype(jnp.bfloat16), "dp").astype(jnp.float32),
        lax.psum(grad_w_out.astype(jnp.bfloat16), "dp").astype(jnp.float32),
        lax.psum(grad_w_gate.astype(jnp.bfloat16), "dp").astype(jnp.float32),
        lax.psum(grad_w_up.astype(jnp.bfloat16), "dp").astype(jnp.float32),
        lax.psum(grad_w_down.astype(jnp.bfloat16), "dp").astype(jnp.float32),
    )
    head_gains = shared[6]
    return (
        block_out,
        grad_inputs,
        grad_w_query,
        shared[0],
        shared[1],
        grad_w_out,
        grad_w_gate,
        grad_w_up,
        grad_w_down,
        shared[2],
        head_gains[:head_size],
        head_gains[head_size:],
        shared[3],
        shared[4],
        shared[5],
    )


def solution(mesh):
    placed = (
        P("dp", "row", "col"),
        P("col", "row"),
        P("col", None),
        P("col", None),
        P("row", "col"),
        P("col", "row"),
        P("col", "row"),
        P("row", "col"),
        P("col"),
        P(),
        P(),
        P("col"),
        P("col"),
        P("col"),
        P("dp", "row", "col"),
    )
    return jax.shard_map(
        local,
        mesh=mesh,
        in_specs=placed,
        out_specs=(
            P("dp", "row", "col"),
            P("dp", "row", "col"),
            P("col", "row"),
            P("col", None),
            P("col", None),
            P("row", "col"),
            P("col", "row"),
            P("col", "row"),
            P("row", "col"),
            P("col"),
            P(),
            P(),
            P("col"),
            P("col"),
            P("col"),
        ),
        check_vma=False,
    )
```

profile of v0, /device:TPU:3, one launch (start us, length us, event | category | flops | bytes accessed | tf_op | source)
XLA Modules:
  0.0 1514.2 jit_solution(17066149595980761530)
XLA Ops:
  26.9 8.2 all-to-all-done.1
  39.7 9.9 reduce.37
  56.7 14.0 all-to-all-done.2
  86.7 7.5 collective-permute-done
  95.6 8.8 collective-permute-done.1
  104.9 14.4 all-gather
  124.5 13.8 all_to_all.147
  138.6 6.4 all_to_all.148
  151.9 14.0 all_to_all.150
  168.3 8.1 reshape.1106
  176.4 11.0 reduce.38
  190.8 13.6 all_to_all.151
  217.8 7.8 convolution_bitcast_fusion
  231.9 71.8 %all-gather.12.cloned.1.call-done = bf16[1,1024,1728]{2,1,0:T(8,128)(2,1)} async-done(((bf16[1,512,1728]{2,1,0:T(8,128)(2,1)}), bf16[1,1024,1728]{2,1,0:T(8,128)(2,1)}) %all-gather.12.cloned.1.call-update) | async-done | bytes 3538960 | tf_op jit(solution)/shard_map/all_gather | solution.py:61
  314.6 18.3 %all_to_all.152 = bf16[4,1,256,576]{2,3,1,0:T(8,128)(2,1)S(1)} all-to-all(bf16[4,1,256,576]{2,3,1,0:T(8,128)(2,1)S(1)} %copy.135), channel_id=1, replica_groups=mesh['dp'=16,'row'=4,'col'=2] {'row'}, dimensions={0} | all-to-all | bytes 2359296 | tf_op jit(solution)/shard_map/all_to_all | solution.py:42
  348.5 16.1 %all_to_all.155 = bf16[4,1,256,576]{2,3,1,0:T(8,128)(2,1)} all-to-all(bf16[4,1,256,576]{2,3,1,0:T(8,128)(2,1)S(1)} %broadcast_in_dim.49), channel_id=1, replica_groups=mesh['dp'=16,'row'=4,'col'=2] {'row'}, dimensions={0} | all-to-all | bytes 2359296 | tf_op jit(solution)/shard_map/all_to_all | solution.py:18
  367.0 8.1 reshape.1108
  375.1 11.0 reduce.39
  389.6 15.1 all_to_all.156
  418.1 9.8 fusion.13
  430.7 97.3 %all-gather.16.cloned.1.call-done = bf16[1,1024,3456]{2,1,0:T(8,128)(2,1)} async-done(((bf16[1,512,3456]{2,1,0:T(8,128)(2,1)}), bf16[1,1024,3456]{2,1,0:T(8,128)(2,1)}) %all-gather.16.cloned.1.call-update) | async-done | bytes 7077904 | tf_op jit(solution)/shard_map/all_gather | solution.py:61
  528.0 9.6 fusion.36
  542.5 18.4 %all_to_all.157 = bf16[4,1,256,576]{2,3,1,0:T(8,128)(2,1)S(1)} all-to-all(bf16[4,1,256,576]{2,3,1,0:T(8,128)(2,1)S(1)} %copy.141), channel_id=1, replica_groups=mesh['dp'=16,'row'=4,'col'=2] {'row'}, dimensions={0} | all-to-all | bytes 2359296 | tf_op jit(solution)/shard_map/all_to_all | solution.py:42
  575.9 14.5 all_to_all.160
  591.9 8.1 reshape.1110
  600.0 9.9 reduce.40
  616.9 16.0 %all_gather.30 = bf16[256,1152]{0,1:T(8,128)(2,1)} all-gather(bf16[256,576]{0,1:T(8,128)(2,1)} %param.19), channel_id=1, replica_groups=mesh['dp'=16,'row'=4,'col'=2] {'col'}, dimensions={1}, use_global_device_ids=true | all-gather | bytes 884736 | tf_op jit(solution)/shard_map/all_gather | solution.py:149
  666.9 7.6 fusion.4
  679.9 23.4 %all-gather.18.cloned.1.call-done = bf16[1,1024,768]{2,1,0:T(8,128)(2,1)} async-done(((bf16[1,512,768]{2,1,0:T(8,128)(2,1)}), bf16[1,1024,768]{2,1,0:T(8,128)(2,1)}) %all-gather.18.cloned.1.call-update) | async-done | bytes 1572880 | tf_op jit(solution)/shard_map/all_gather | solution.py:61
  723.1 12.1 all-to-all-done.18
  739.5 315.1 %all-reduce.4 = (f32[576]{0:T(1024)}, f32[512]{0:T(512)S(1)}, f32[576]{0:T(1024)}, f32[576]{0:T(1024)}, f32[576]{0:T(1024)}) all-reduce(f32[576]{0:T(1024)S(1)} %get-tuple-element.29, f32[512]{0:T(512)S(1)} %reduce_sum.362, f32[576]{0:T(1024)S(1)} %get-tuple-element.25, ...), channel_id=1, replica_groups=mesh['dp'=16,'row'=4,'col'=2] {'dp','row'}, use_global_device_ids=true, to_apply=%region_35.36 | all-reduce | flops 2816 | bytes 22528 | tf_op jit(solution)/shard_map/psum | solution.py:342
  1068.4 434.7 %all-reduce.10.cloned.1.call-done = (f32[576,256]{1,0:T(8,128)}, f32[576,256]{1,0:T(8,128)}) async-done(((f32[576,256]{1,0:T(8,128)}, f32[576,256]{1,0:T(8,128)}), (f32[576,256]{1,0:T(8,128)}, f32[576,256]{1,0:T(8,128)})) %all-reduce.10.cloned.1.call-update) | async-done | bytes 1179664 | tf_op jit(solution)/shard_map/psum | solution.py:342
  (272 shorter events, 243.9 us)
Async XLA Ops:
  7.2 71.2 %all-gather.8.cloned.1.call-start = ((), (), s32[]{:S(2)}) async-start(), calls=%async_computation.21 | async-start | bytes 2654208 | tf_op jit(solution)/shard_map/all_gather | solution.py:147
  17.9 17.2 %all-to-all-start.1 = ((bf16[4,1,256,576]{2,3,1,0:T(8,128)(2,1)}), bf16[4,1,256,576]{2,3,1,0:T(8,128)(2,1)S(1)}, u32[]{:S(2)}, u32[]{:S(2)}) async-start(bf16[4,1,256,576]{2,3,1,0:T(8,128)(2,1)} %broadcast_in_dim.41), calls=%async_computation.1 | async-start | bytes 2359296 | tf_op jit(solution)/shard_map/all_to_all | solution.py:18
  22.2 195.6 %all-gather.10.cloned.1.call-start = ((), (), s32[]{:S(2)}) async-start(), calls=%async_computation.22 | async-start | bytes 11943936 | tf_op jit(solution)/shard_map/all_gather | solution.py:148
  52.0 18.8 %all-to-all-start.2 = ((bf16[2,2,147456]{2,1,0:T(2,128)(2,1)}), bf16[2,2,147456]{2,1,0:T(2,128)(2,1)}, u32[]{:S(2)}, u32[]{:S(2)}) async-start(bf16[2,2,147456]{2,1,0:T(2,128)(2,1)} %reshape.1112), calls=%async_computation.2 | async-start | bytes 2359296 | tf_op jit(solution)/shard_map/all_to_all | solution.py:69
  56.4 247.2 %all-gather.12.cloned.1.call-start = ((), (), s32[]{:S(2)}) async-start(), calls=%async_computation.23 | async-start | bytes 5505024 | tf_op jit(solution)/shard_map/all_gather | solution.py:61
  82.9 12.2 copy-start.25
  82.9 12.2 copy-start.27
  83.0 12.1 copy-start.34
  83.0 11.2 collective-permute-start
  85.4 19.0 %copy-start.29 = (bf16[1,512,256]{2,1,0:T(8,128)(2,1)}, bf16[1,512,256]{2,1,0:T(8,128)(2,1)S(1)}, u32[]{:S(2)}) copy-start(bf16[1,512,256]{2,1,0:T(8,128)(2,1)S(1)} %slice.152) | copy-start | bytes 786436
  85.4 19.0 %collective-permute-start.1 = (bf16[1,512,256]{2,1,0:T(8,128)(2,1)S(1)}, bf16[1,512,256]{2,1,0:T(8,128)(2,1)S(1)}, u32[]{:S(2)}, u32[]{:S(2)}) collective-permute-start(bf16[1,512,256]{2,1,0:T(8,128)(2,1)S(1)} %slice.152), channel_id=1, source_target_pairs={{0,1},{2,3},{4,5},{6,7},{8,9},{10,11},{12,13},{14,15},{16,17},{18,... | collective-permute-start | bytes 786440 | tf_op jit(solution)/shard_map/ppermute | solution.py:49
  95.6 24.5 %copy-start.24 = (bf16[256,576]{0,1:T(8,128)(2,1)S(1)}, bf16[256,576]{0,1:T(8,128)(2,1)}, u32[]{:S(2)}) copy-start(bf16[256,576]{0,1:T(8,128)(2,1)} %param.19) | copy-start | bytes 884740
  104.4 14.9 copy-start.32
  124.5 20.6 %copy-start.37 = (f32[576]{0:T(1024)S(1)}, f32[576]{0:T(1024)}, u32[]{:S(2)}) copy-start(f32[576]{0:T(1024)} %param.26) | copy-start | bytes 6916
  138.4 13.3 copy-start.36
  231.2 186.8 %all-gather.14.cloned.1.call-start = ((), (), s32[]{:S(2)}) async-start(), calls=%async_computation.24 | async-start | bytes 6193152 | tf_op jit(solution)/shard_map/all_gather | solution.py:150
  231.8 296.2 %all-gather.16.cloned.1.call-start = ((), (), s32[]{:S(2)}) async-start(), calls=%async_computation.25 | async-start | bytes 10616832 | tf_op jit(solution)/shard_map/all_gather | solution.py:61
  314.6 24.8 %copy-start.39 = (f32[576]{0:T(1024)S(1)}, f32[576]{0:T(1024)}, u32[]{:S(2)}) copy-start(f32[576]{0:T(1024)} %param.28) | copy-start | bytes 6916
  590.4 9.5 copy-start.5
  612.3 20.6 %copy-start.3 = (bf16[4,1,256,576]{2,3,1,0:T(8,128)(2,1)S(1)}, bf16[4,1,256,576]{2,3,1,0:T(8,128)(2,1)}, u32[]{:S(2)}) copy-start(bf16[4,1,256,576]{2,3,1,0:T(8,128)(2,1)} %copy-done.2) | copy-start | bytes 3538948
  612.3 30.7 %all-to-all-start.17 = ((bf16[2,2,147456]{2,1,0:T(2,128)(2,1)}), bf16[2,2,147456]{2,1,0:T(2,128)(2,1)}, u32[]{:S(2)}, u32[]{:S(2)}) async-start(bf16[2,2,147456]{2,1,0:T(2,128)(2,1)} %reshape.1118), calls=%async_computation.17 | async-start | bytes 2359296 | tf_op jit(solution)/shard_map/all_to_all | solution.py:69
  616.9 86.5 %all-gather.18.cloned.1.call-start = ((), (), s32[]{:S(2)}) async-start(), calls=%async_computation.26 | async-start | bytes 2359296 | tf_op jit(solution)/shard_map/all_gather | solution.py:61
  655.5 7.2 collective-permute-start.2
  657.6 8.0 collective-permute-start.3
  666.6 389.6 %all-reduce.12.cloned.1.call-start = ((), (), s32[]{:S(2)}) async-start(), calls=%async_computation.28 | async-start | bytes 13565952 | tf_op jit(solution)/shard_map/psum | solution.py:355
  678.5 24.9 %copy-start.22 = (bf16[72,8,4,256]{3,1,2,0:T(8,128)(2,1)S(1)}, bf16[72,8,4,256]{3,1,2,0:T(8,128)(2,1)}, u32[]{:S(2)}) copy-start(bf16[72,8,4,256]{3,1,2,0:T(8,128)(2,1)} %copy.176) | copy-start | bytes 3538948
  708.5 8.0 all-to-all-start.20
  716.4 18.8 %all-to-all-start.18 = ((bf16[4,1,256,576]{2,3,1,0:T(8,128)(2,1)}), bf16[4,1,256,576]{2,3,1,0:T(8,128)(2,1)S(1)}, u32[]{:S(2)}, u32[]{:S(2)}) async-start(bf16[4,1,256,576]{2,3,1,0:T(8,128)(2,1)} %copy.149), calls=%async_computation.18 | async-start | bytes 2359296 | tf_op jit(solution)/shard_map/all_to_all | solution.py:42
  720.7 14.7 copy-start.11
  720.7 782.4 %all-reduce.10.cloned.1.call-start = ((), (), s32[]{:S(2)}) async-start(), calls=%async_computation.27 | async-start | bytes 2359296 | tf_op jit(solution)/shard_map/psum | solution.py:342
  723.1 332.1 %copy-start.13 = (f32[1,256,576]{1,2,0:T(8,128)S(1)}, f32[1,256,576]{1,2,0:T(8,128)}, u32[]{:S(2)}) copy-start(f32[1,256,576]{1,2,0:T(8,128)} %get-tuple-element.43) | copy-start | bytes 1769476
  736.3 318.9 %all-to-all-start.19 = ((f32[2,1,256,1]{2,3,1,0:T(1,128)}), f32[2,1,256,1]{2,3,1,0:T(1,128)S(1)}, u32[]{:S(2)}, u32[]{:S(2)}) async-start(f32[2,1,256,1]{2,3,1,0:T(1,128)} %broadcast_in_dim.55), calls=%async_computation.19 | async-start | bytes 4096 | tf_op jit(solution)/shard_map/all_to_all | solution.py:18
  (31 other events, 83.8 us)
Sparse Core Ops, SparseCore 0:
  11.3 34.3 all-gather.7
  47.9 124.1 all-gather.9
  231.4 72.2 all-gather.11
  305.2 59.6 all-gather.13
  430.8 97.1 all-gather.15
  666.7 36.6 all-gather.17
  708.0 176.9 all-reduce.11
  888.0 615.0 all-reduce.9
where the time goes:
time: 1530 us; the launch traced here: 1510 us
  waiting for transfers between devices  683 us (45%)
  blocking collectives  507 us (33%)
  local copies, waits for them, and re-layouts  138 us (9%)
  other arithmetic  81.1 us (5%)
  matrix products  59 us (4%)
  starting transfers between devices  31.1 us (2%)
  between operations  15.5 us (1%)
    psum x1, waiting for transfers between devices, local(): lax.psum((grad_w_key, grad_w_value, grad_g_in, grad_g_post_attn, grad_g_p...  435 us
    psum x1, blocking collectives, local(): lax.psum((grad_w_key, grad_w_value, grad_g_in, grad_g_post_attn, grad_g_p...  315 us
    all_gather x3, waiting for transfers between devices, col_gather(): return lax.all_gather(values, 'col', axis=1, tiled=True)  193 us
    all_to_all x10, blocking collectives, sent_to_all(): return lax.all_to_all(copies, axis, split_axis=0, concat_axis=0, tiled=True)  82.5 us
    unnamed x111, local copies, waits for them, and re-layouts  54.6 us
    all_to_all x3, blocking collectives, summed_on_arrival(): lax.all_to_all(cut_along(shard, dim, length), axis, 0, 0, tiled=True)  50.6 us
    unnamed x4, other arithmetic  41.8 us
    another operation x8, local copies, waits for them, and re-layouts, laid_out(): return jnp.moveaxis(parts, 0, dim).reshape(shape)  34.5 us
  transfers between devices with their start and end apart: 18, of which 11 were waited for; matrix products, arithmetic and copies ran while one was open for 12% of the time, Pallas kernels for 0%

commit v1 on v0

v1 whole, which is shorter than its diff:
```python
import jax
import jax.numpy as jnp
import numpy as np
from jax import lax
from jax.sharding import PartitionSpec as P

WINDOW = 512
EPSILON = 1e-06
MASKED = -1e30
ROPE_BASE = 10000.0
LOW = jnp.bfloat16
WIDE = jnp.float32

Y, HI, CORE, COL, ROW = 4, 2, 2, 2, 4


def device(y, z, core):
    return ((y * HI + z // COL) * CORE + core) * COL + z % COL


def z_route(shift_of):
    return [
        (device(y, z, core), device(y, (z + shift_of(z, core)) % 4, core))
        for y in range(Y)
        for z in range(4)
        for core in range(CORE)
    ]


def dp_route(target):
    return [(i, target(i)) for i in range(Y * HI * CORE)]


def by_z(shift_of):
    route = z_route(shift_of)
    return lambda v: lax.ppermute(v, ("dp", "col"), route)


to_partner = by_z(lambda z, core: 1 if z % 2 == 0 else -1)
to_cross = by_z(lambda z, core: -1 if z % 2 == 0 else 1)
to_opposite = by_z(lambda z, core: 2)
z_ring = by_z(lambda z, core: -1 if core == 0 else 1)


def core_swap(v):
    return lax.ppermute(v, "dp", dp_route(lambda i: i ^ 1))


def y_ring(v):
    step = HI * CORE
    return lax.ppermute(
        v, "dp", dp_route(lambda i: (i + (step if i % 2 == 0 else -step)) % (Y * step))
    )


def y_shift(v, distance):
    step = HI * CORE * distance
    return lax.ppermute(v, "dp", dp_route(lambda i: (i + step) % (Y * HI * CORE)))


def row_shift(v, distance):
    return lax.ppermute(v, "row", [(i, (i + distance) % ROW) for i in range(ROW)])


def row_gather(v):
    return jnp.concatenate([v, row_shift(v, 1), row_shift(v, -1), row_shift(v, 2)], axis=1)


def row_scatter(total):
    share = total.shape[1] // ROW
    own, *others = [total[:, i * share : (i + 1) * share] for i in range(ROW)]
    for part, distance in ((others[2], 2), (others[0], -1), (others[1], 1)):
        own = own + row_shift(part.astype(LOW), distance).astype(WIDE)
    return own


def dot(left, right, dims):
    return lax.dot_general(left, right, (dims, ((), ())), preferred_element_type=WIDE)


def norm(v, gain):
    factor = lax.rsqrt(jnp.sum(v * v, axis=0, keepdims=True) / v.shape[0] + EPSILON)
    return v * factor * gain, factor


def norm_back(v, factor, gain, upstream):
    scaled = upstream * gain
    inner = jnp.sum(scaled * v, axis=0, keepdims=True)
    grad = factor * scaled - v * (factor * factor * factor) * inner / v.shape[0]
    return grad, jnp.sum(upstream * v * factor, axis=1)


def head_map(raw, gain, cosine, sine, scaling):
    normed = (
        raw * lax.rsqrt(jnp.mean(raw * raw, axis=0, keepdims=True) + EPSILON) * gain[:, None]
    )
    half = raw.shape[0] // 2
    first, second = normed[:half], normed[half:]
    turned = jnp.concatenate(
        [first * cosine - second * sine, second * cosine + first * sine], axis=0
    )
    return turned * scaling


def geglu(gate, up):
    return jax.nn.gelu(gate, approximate=True) * up


def rope_tables(length, head_size):
    half = head_size // 2
    exponent = np.arange(half, dtype=np.float32) * np.float32(2.0 / head_size)
    rate = np.float32(ROPE_BASE) ** (-exponent)
    angles = rate[:, None] * np.arange(length, dtype=np.float32)[None, :]
    return np.stack([np.cos(angles), np.sin(angles)]).astype(np.float32)


def pick(v, index, axis):
    return lax.dynamic_index_in_dim(v, index, axis, keepdims=False)


def fetch(own, core):
    half = own.shape[0] // 2
    mine = z_ring(lax.dynamic_slice_in_dim(own, core * half, half, 0))
    return mine


def assemble(own, mine, core):
    theirs = core_swap(mine)
    first = jnp.where(core == 0, mine, theirs)
    second = jnp.where(core == 0, theirs, mine)
    return jnp.concatenate([own, first, second], axis=0)


def add(a, b):
    return (a.astype(WIDE) + b.astype(WIDE)).astype(LOW)


def reduce_weight(grad, place):
    y, hi, core = place
    width = grad.shape[1]
    parts = grad.reshape(COL, CORE, -1, width)
    held = add(pick(parts, core, 1), core_swap(pick(parts, 1 - core, 1)))
    chunks = held.reshape(COL, Y, -1, width)
    way = 1 - 2 * core

    def chunk(steps):
        return pick(chunks, (y - steps * way) % Y, 1)

    total = chunk(1)
    for step in range(Y - 1):
        total = add(y_ring(total), chunk(step + 2))
    halves = total.reshape(COL, -1, HI, width // HI)
    near, far = pick(halves, hi, 2), pick(halves, 1 - hi, 2)
    piece = (
        near[0].astype(WIDE)
        + to_partner(near[1]).astype(WIDE)
        + to_cross(far[1]).astype(WIDE)
        + to_opposite(far[0]).astype(WIDE)
    ).astype(LOW)
    other = to_opposite(piece)
    piece = jnp.where(
        hi == 0,
        jnp.concatenate([piece, other], axis=1),
        jnp.concatenate([other, piece], axis=1),
    )
    ring = [piece]
    for step in range(Y - 1):
        ring.append(y_ring(ring[-1]))
    ring = jnp.stack(ring)
    mine = jnp.concatenate([pick(ring, (way * (y - j)) % Y, 0) for j in range(Y)], axis=0)
    theirs = core_swap(mine)
    return jnp.where(
        core == 0,
        jnp.concatenate([mine, theirs], axis=0),
        jnp.concatenate([theirs, mine], axis=0),
    )


def reduce_gains(gains):
    total = gains + core_swap(gains)
    total = total + y_shift(total, 1) + y_shift(total, 2) + y_shift(total, 3)
    total = total + row_shift(total, 1) + row_shift(total, 2) + row_shift(total, 3)
    total = total + to_opposite(total)
    theirs = to_partner(total)
    return (total + jnp.concatenate([theirs[::-1, :4], theirs[:, 4:]], axis=1))


def local(
    inputs,
    w_query,
    w_key,
    w_value,
    attention_output_weight,
    w_gate,
    w_up,
    down_weight,
    g_in,
    g_query,
    g_key,
    g_post_attn,
    g_pre_ffn,
    g_post_ffn,
    cotangent,
):
    col, row, dp = lax.axis_index("col"), lax.axis_index("row"), lax.axis_index("dp")
    core, hi, y = dp % CORE, (dp // CORE) % HI, dp // (HI * CORE)
    place = (y, hi, core)
    features, share = inputs.shape[2], inputs.shape[1] // COL
    head = g_query.shape[0]
    hidden_share = w_gate.shape[1]
    padding = -hidden_share % 256
    barrier = lax.optimization_barrier

    def spread(v):
        kept = lax.dynamic_slice_in_dim(v, col * share, share, 1)
        given = lax.dynamic_slice_in_dim(v, (1 - col) * share, share, 1)
        return kept, to_partner(given)

    def back_together(v):
        kept, given = v[:features], v[features:]
        theirs = to_partner(given)
        return jnp.where(
            col == 0,
            jnp.concatenate([kept, theirs], axis=1),
            jnp.concatenate([theirs, kept], axis=1),
        )

    gains_own = jnp.stack([g_in, g_post_attn, g_pre_ffn, g_post_ffn])
    gains = jnp.concatenate([gains_own, to_partner(gains_own)], axis=1).T
    gain_in, gain_post_attn, gain_pre_ffn, gain_post_ffn = [gains[:, i : i + 1] for i in range(4)]

    kept, taken = spread(inputs[0].T)
    attn_own = jnp.concatenate([w_query, w_key, w_value, attention_output_weight.T], axis=1)
    attn_own, taken = barrier((attn_own, taken))
    attn_weight = assemble(attn_own, fetch(attn_own, core), core)
    qkv_weight, out_weight = attn_weight[:, : 3 * head], attn_weight[:, 3 * head :]

    pad = lambda w: jnp.pad(w, ((0, 0), (0, padding)))
    ffn_own = jnp.concatenate([pad(w_gate), pad(w_up), pad(down_weight.T)], axis=1)
    wide = hidden_share + padding
    ffn_mine = fetch(barrier((ffn_own, taken))[0], core)

    x = jnp.concatenate([kept, taken], axis=0).astype(WIDE)
    attn_norm, attn_factor = norm(x, gain_in)
    attn_in = row_gather(attn_norm.astype(LOW))
    qkv = dot(qkv_weight, attn_in, ((0,), (0,)))
    raw_query, raw_key, value = qkv[:head], qkv[head : 2 * head], qkv[2 * head :].astype(LOW)

    chunk_rows = [row, (row - 1) % ROW, (row + 1) % ROW, (row + 2) % ROW]
    tables = jnp.asarray(rope_tables(ROW * COL * share, head))
    turns = jnp.concatenate(
        [
            lax.dynamic_slice_in_dim(tables, (r * COL + col) * share, share, 2)
            for r in chunk_rows
        ],
        axis=2,
    )
    cosine, sine = turns[0], turns[1]
    query_rot, query_pull = jax.vjp(
        lambda v, g: head_map(v, g, cosine, sine, head**-0.5), raw_query, g_query
    )
    key_rot, key_pull = jax.vjp(lambda v, g: head_map(v, g, cosine, sine, 1.0), raw_key, g_key)
    query_low = query_rot.astype(LOW)
    key_value = jnp.concatenate([key_rot.astype(LOW), value], axis=0)
    key_value = jnp.concatenate([key_value, to_partner(key_value)], axis=1)
    key_all, value_all = key_value[:head], key_value[head:]

    within = jnp.arange(share, dtype=jnp.int32)
    position = lambda c: jnp.concatenate([(r * COL + c) * share + within for r in chunk_rows])
    query_position = position(col)
    key_position = jnp.concatenate([query_position, position(1 - col)])
    offset = query_position[None, :] - key_position[:, None]
    allowed = (offset >= 0) & (offset < WINDOW)
    scores = jnp.where(allowed, dot(key_all, query_low, ((0,), (0,))), MASKED)
    weights = jnp.exp(scores - jnp.max(scores, axis=0, keepdims=True))
    probs = weights / jnp.sum(weights, axis=0, keepdims=True)
    probs_low = probs.astype(LOW)
    mixed = dot(value_all, probs_low, ((1,), (0,))).astype(LOW)
    branch = row_scatter(dot(out_weight, mixed, ((1,), (0,))))
    post_attn, post_factor = norm(branch, gain_post_attn)
    middle = x + post_attn
    ffn_norm, ffn_factor = norm(middle, gain_pre_ffn)
    ffn_in = row_gather(ffn_norm.astype(LOW))

    ffn_weight = assemble(ffn_own, ffn_mine, core)
    gate_weight, up_weight, down_t = [ffn_weight[:, i * wide : (i + 1) * wide] for i in range(3)]
    gate = dot(gate_weight, ffn_in, ((0,), (0,)))
    up = dot(up_weight, ffn_in, ((0,), (0,)))
    hidden, geglu_pull = jax.vjp(geglu, gate, up)
    hidden = hidden.astype(LOW)
    down_proj = row_scatter(dot(down_t, hidden, ((1,), (0,))))
    post_ffn, post_ffn_factor = norm(down_proj, gain_post_ffn)
    block_out = back_together((middle + post_ffn).astype(LOW))

    upstream = jnp.concatenate(spread(cotangent[0].T), axis=0).astype(WIDE)
    grad_down, grad_g_post_ffn = norm_back(down_proj, post_ffn_factor, gain_post_ffn, upstream)
    grad_down = row_gather(grad_down.astype(LOW))
    grad_gate, grad_up = geglu_pull(dot(down_t, grad_down, ((0,), (0,))))
    grad_gate, grad_up = grad_gate.astype(LOW), grad_up.astype(LOW)
    grad_ffn_in = row_scatter(
        dot(gate_weight, grad_gate, ((1,), (0,))) + dot(up_weight, grad_up, ((1,), (0,)))
    )
    grad_w_down = reduce_weight(dot(grad_down, hidden, ((1,), (1,))).astype(LOW), place)
    grad_w_gate = reduce_weight(dot(ffn_in, grad_gate, ((1,), (1,))).astype(LOW), place)
    grad_w_up = reduce_weight(dot(ffn_in, grad_up, ((1,), (1,))).astype(LOW), place)

    grad_mid_norm, grad_g_pre_ffn = norm_back(middle, ffn_factor, gain_pre_ffn, grad_ffn_in)
    grad_middle = upstream + grad_mid_norm
    grad_branch, grad_g_post_attn = norm_back(branch, post_factor, gain_post_attn, grad_middle)
    grad_branch = row_gather(grad_branch.astype(LOW))
    grad_w_out = dot(grad_branch, mixed, ((1,), (1,))).astype(LOW)
    grad_mixed = dot(out_weight, grad_branch, ((0,), (0,))).astype(LOW)

    grad_probs = dot(value_all, grad_mixed, ((0,), (0,)))
    grad_value_all = dot(grad_mixed, probs_low, ((1,), (1,)))
    grad_scores = (
        probs * (grad_probs - jnp.sum(probs * grad_probs, axis=0, keepdims=True))
    ).astype(LOW)
    grad_query_rot = dot(key_all, grad_scores, ((1,), (0,)))
    grad_key_all = dot(query_low, grad_scores, ((1,), (1,)))
    grad_kv_all = jnp.concatenate([grad_key_all, grad_value_all], axis=0)
    count = grad_kv_all.shape[1] // 2
    grad_kv = grad_kv_all[:, :count] + to_partner(grad_kv_all[:, count:].astype(LOW)).astype(WIDE)
    grad_query, grad_g_query = query_pull(grad_query_rot)
    grad_key, grad_g_key = key_pull(grad_kv[:head])
    grad_query = grad_query.astype(LOW)
    grad_kv = jnp.concatenate([grad_key, grad_kv[head:]], axis=0).astype(LOW)
    grad_qkv = jnp.concatenate([grad_query, grad_kv], axis=0)

    grad_attn_part = dot(qkv_weight, grad_qkv, ((1,), (0,)))
    grad_attn_in = row_scatter(grad_attn_part)
    grad_in_norm, _ = norm_back(x, attn_factor, gain_in, grad_attn_in)
    grad_inputs = back_together((grad_middle + grad_in_norm).astype(LOW))
    grad_g_in = jnp.sum(grad_attn_part * attn_in.astype(WIDE), axis=1) / gain_in[:, 0]

    quarters = grad_kv.reshape(ROW, -1, count)
    quarter = pick(quarters, row, 0).astype(WIDE)
    order = (0, -1, 1, 2)
    for distance in (1, 2, 3):
        given = row_shift(pick(quarters, (row + distance) % ROW, 0), distance)
        theirs = [(step - distance) % ROW for step in order]
        chunks = [given[:, i * share : (i + 1) * share] for i in range(ROW)]
        chunks = [chunks[theirs.index(step % ROW)] for step in order]
        quarter = quarter + jnp.concatenate(chunks, axis=1).astype(WIDE)
    grad_last = jnp.concatenate(
        [
            grad_w_out,
            dot(attn_in, jnp.concatenate([grad_query, quarter.astype(LOW)], axis=0), ((1,), (1,))).astype(LOW),
        ],
        axis=1,
    )
    slack = -grad_last.shape[1] % 256
    grad_last = reduce_weight(jnp.pad(grad_last, ((0, 0), (0, slack))), place)
    grad_w_out = grad_last[:, :head]
    grad_w_query = grad_last[:, head : 2 * head]
    quarter = grad_last[:, 2 * head : 2 * head + 2 * head // ROW]
    by_row = jnp.stack(
        [quarter, row_shift(quarter, 1), row_shift(quarter, 2), row_shift(quarter, 3)]
    )
    grad_w_kv = jnp.concatenate([pick(by_row, (row - r) % ROW, 0) for r in range(ROW)], axis=1)

    feature_gains = jnp.stack([grad_g_in, grad_g_post_attn, grad_g_pre_ffn, grad_g_post_ffn])
    head_gains = jnp.stack([grad_g_query, grad_g_key])
    head_gains = jnp.pad(head_gains, ((0, 0), (0, features - head)))
    summed = reduce_gains(
        jnp.concatenate(
            [feature_gains.reshape(4, COL, features).swapaxes(0, 1), head_gains[:, None]], axis=1
        )
    )

    whole = lambda w: w[:, :hidden_share].astype(WIDE)
    return (
        block_out.T[None],
        grad_inputs.T[None],
        grad_w_query.astype(WIDE),
        grad_w_kv[:, :head].astype(WIDE),
        grad_w_kv[:, head:].astype(WIDE),
        grad_w_out.astype(WIDE).T,
        whole(grad_w_gate),
        whole(grad_w_up),
        whole(grad_w_down).T,
        summed[0, 0],
        summed[0, 4, :head],
        summed[1, 4, :head],
        summed[0, 1],
        summed[0, 2],
        summed[0, 3],
    )


def solution(mesh):
    placed = (
        P("dp", "row", "col"),
        P("col", "row"),
        P("col", None),
        P("col", None),
        P("row", "col"),
        P("col", "row"),
        P("col", "row"),
        P("row", "col"),
        P("col"),
        P(),
        P(),
        P("col"),
        P("col"),
        P("col"),
        P("dp", "row", "col"),
    )
    return jax.shard_map(
        local,
        mesh=mesh,
        in_specs=placed,
        out_specs=(
            P("dp", "row", "col"),
            P("dp", "row", "col"),
            P("col", "row"),
            P("col", None),
            P("col", None),
            P("row", "col"),
            P("col", "row"),
            P("col", "row"),
            P("row", "col"),
            P("col"),
            P(),
            P(),
            P("col"),
            P("col"),
            P("col"),
        ),
        check_vma=False,
    )
```

time: 1530 us -> 494 us (0.32)
  waiting for transfers between devices: 683 us -> 134 us
  blocking collectives: 507 us -> 0 us
  starting transfers between devices: 31.1 us -> 160 us
  local copies, waits for them, and re-layouts: 138 us -> 44.1 us
    psum x2 -> x0, waiting for transfers between devices: 435 us -> none  [the longest x1 435 us: local(): lax.psum((grad_w_key, grad_w_value, grad_g_in, grad_g_post_attn, grad_g_p...]
    psum x1 -> x0, blocking collectives: 315 us -> none  [local(): lax.psum((grad_w_key, grad_w_value, grad_g_in, grad_g_post_attn, grad_g_p...]
    all_gather x6 -> x0, waiting for transfers between devices: 193 us -> none  [the longest x3 193 us: col_gather(): return lax.all_gather(values, 'col', axis=1, tiled=True)]
    all_to_all x15 -> x0, blocking collectives: 162 us -> none  [the longest x10 82.5 us: sent_to_all(): return lax.all_to_all(copies, axis, split_axis=0, concat_axis=0, tiled=True)]
    ppermute x4 -> x98, starting transfers between devices: 6.39 us -> 160 us  [the longest x11 48.9 us: core_swap(): return lax.ppermute(v, 'dp', dp_route(lambda i: i ^ 1))]
    ppermute x4 -> x98, waiting for transfers between devices: 20.3 us -> 134 us  [the longest x33 64.1 us: row_shift(): lax.ppermute(v, 'row', [(i, (i + distance) % ROW) for i in range(ROW)])]
    another operation x16 -> x8, local copies, waits for them, and re-layouts: 49.4 us -> 3.6 us  [the longest x4 2.75 us: local(): gains_own = jnp.stack([g_in, g_post_attn, g_pre_ffn, g_post_ffn])]
    unnamed x4 -> x9, other arithmetic: 41.8 us -> 0.05 us
  transfers between devices with their start and end apart: 18 -> 98, of which waited for: 11 -> 36; matrix products, arithmetic and copies ran while one was open for 12% -> 29% of each run, Pallas kernels for 0% -> 0%
where the time goes in v1:
time: 494 us; the launch traced here: 484 us
  starting transfers between devices  160 us (32%)
  waiting for transfers between devices  134 us (27%)
  other arithmetic  93.8 us (19%)
  matrix products  48.4 us (10%)
  local copies, waits for them, and re-layouts  44.1 us (9%)
    ppermute x33, waiting for transfers between devices, row_shift(): lax.ppermute(v, 'row', [(i, (i + distance) % ROW) for i in range(ROW)])  64.1 us
    ppermute x11, starting transfers between devices, core_swap(): return lax.ppermute(v, 'dp', dp_route(lambda i: i ^ 1))  48.9 us
    dot_general x21, matrix products, dot(): lax.dot_general(left, right, (dims, ((), ())), preferred_element_type=WIDE)  48.4 us
    ppermute x33, starting transfers between devices, row_shift(): lax.ppermute(v, 'row', [(i, (i + distance) % ROW) for i in range(ROW)])  42.1 us
    concatenate x1, other arithmetic, assemble(): return jnp.concatenate([own, first, second], axis=0)  36.9 us
    ppermute x24, starting transfers between devices, y_ring(): lax.ppermute(v, 'dp', dp_route(lambda i: (i + (step if i % 2 == 0 else -s...  36.1 us
    ppermute x27, waiting for transfers between devices, by_z(): return lambda v: lax.ppermute(v, ('dp', 'col'), route)  34.1 us
    ppermute x24, waiting for transfers between devices, y_ring(): lax.ppermute(v, 'dp', dp_route(lambda i: (i + (step if i % 2 == 0 else -s...  31.8 us
  transfers between devices with their start and end apart: 98, of which 36 were waited for; matrix products, arithmetic and copies ran while one was open for 29% of the time, Pallas kernels for 0%

profile of v1, /device:TPU:3, one launch (start us, length us, event | category | flops | bytes accessed | tf_op | source)
XLA Modules:
  0.0 484.2 jit_solution(7044184484171862018)
XLA Ops:
  13.0 5.4 %pad_maximum_fusion.1 = bf16[576,5376]{1,0:T(8,128)(2,1)} fusion(bf16[576,1792]{1,0:T(8,128)(2,1)S(1)} %pad.32, bf16[576,1792]{1,0:T(8,128)(2,1)} %pad.31, bf16[576,1792]{1,0:T(8,128)(2,1)} %pad.30), kind=kLoop, calls=%fused_computation.4 | loop fusion | flops 18579456 | bytes 12386304 | tf_op jit(solution)/shard_map/concatenate | solution.py:239
  24.0 3.7 constant_dynamic-slice_fusion.14
  29.6 3.9 collective-permute-done.1
  41.1 6.0 %collective-permute-done.6 = bf16[1152,128]{1,0:T(8,128)(2,1)} collective-permute-done((bf16[1152,128]{1,0:T(8,128)(2,1)}, bf16[1152,128]{1,0:T(8,128)(2,1)}, u32[]{:S(2)}, u32[]{:S(2)}) %collective-permute-start.6) | collective-permute-done | bytes 294944 | tf_op jit(solution)/shard_map/ppermute | solution.py:62
  47.1 6.6 %collective-permute-done.5 = bf16[1152,128]{1,0:T(8,128)(2,1)} collective-permute-done((bf16[1152,128]{1,0:T(8,128)(2,1)}, bf16[1152,128]{1,0:T(8,128)(2,1)}, u32[]{:S(2)}, u32[]{:S(2)}) %collective-permute-start.5) | collective-permute-done | bytes 294944 | tf_op jit(solution)/shard_map/ppermute | solution.py:62
  58.4 16.9 %collective-permute-done.7 = bf16[512,512]{1,0:T(8,128)(2,1)S(1)} collective-permute-done((bf16[512,512]{1,0:T(8,128)(2,1)S(1)}, bf16[512,512]{1,0:T(8,128)(2,1)S(1)}, u32[]{:S(2)}, u32[]{:S(2)}) %collective-permute-start.7) | collective-permute-done | bytes 524320 | tf_op jit(solution)/shard_map/ppermute | solution.py:36
  76.2 4.4 collective-permute-start.12
  85.8 5.0 %collective-permute-done.10 = bf16[1152,128]{1,0:T(8,128)(2,1)S(1)} collective-permute-done((bf16[1152,128]{1,0:T(8,128)(2,1)S(1)}, bf16[1152,128]{1,0:T(8,128)(2,1)S(1)}, u32[]{:S(2)}, u32[]{:S(2)}) %collective-permute-start.10) | collective-permute-done | bytes 294944 | tf_op jit(solution)/shard_map/ppermute | solution.py:62
  91.7 7.0 %collective-permute-done.8 = bf16[1152,128]{1,0:T(8,128)(2,1)S(1)} collective-permute-done((bf16[1152,128]{1,0:T(8,128)(2,1)S(1)}, bf16[1152,128]{1,0:T(8,128)(2,1)S(1)}, u32[]{:S(2)}, u32[]{:S(2)}) %collective-permute-start.8) | collective-permute-done | bytes 294944 | tf_op jit(solution)/shard_map/ppermute | solution.py:62
  103.5 3.9 broadcast_select_fusion.1
  107.5 36.9 %pad_maximum_fusion = bf16[1152,5376]{1,0:T(8,128)(2,1)S(1)} fusion(bf16[288,5376]{1,0:T(8,128)(2,1)} %get-tuple-element.86, bf16[288,5376]{1,0:T(8,128)(2,1)S(1)} %get-tuple-element.85, bf16[576,1792]{1,0:T(8,128)(2,1)S(1)} %pad.32, bf16[576,1792]{1,0:T(8,128)(2,1)S(1)} %copy-done, bf16[576,1792]{1,0:T(8,128)(2,1)S(1)} %copy-done.1), kind=kLoop, calls=%fused_computation | loop fusion | flops 61931520 | bytes 24772608 | tf_op jit(solution)/shard_map/concatenate | solution.py:131
  147.5 5.3 %multiply_convert_fusion.1 = (bf16[1792,512]{1,0:T(8,128)(2,1)S(1)}, f32[1792,512]{1,0:T(8,128)}) fusion(f32[1792,512]{1,0:T(8,128)S(1)} %fusion.16, bf16[1152,128]{1,0:T(8,128)(2,1)S(1)} %collective-permute-done.15, bf16[1152,128]{1,0:T(8,128)(2,1)S(1)} %collective-permute-done.14, bf16[1152,128]{1,0:T(8,128)(2,1)S(1)} %collective-permute-done.13, ...), kind=kOutput, calls=%fused_computation.22 | convolution fusion | flops 2127822848 | bytes 14483456 | tf_op jit(solution)/shard_map/dot_general | solution.py:78
  163.4 7.2 %collective-permute-done.16 = bf16[1152,128]{1,0:T(8,128)(2,1)S(1)} collective-permute-done((bf16[1152,128]{1,0:T(8,128)(2,1)S(1)}, bf16[1152,128]{1,0:T(8,128)(2,1)S(1)}, u32[]{:S(2)}, u32[]{:S(2)}) %collective-permute-start.16) | collective-permute-done | bytes 294944 | tf_op jit(solution)/shard_map/ppermute | solution.py:62
  178.9 7.1 %collective-permute-done.22 = bf16[1152,128]{1,0:T(8,128)(2,1)S(1)} collective-permute-done((bf16[1152,128]{1,0:T(8,128)(2,1)S(1)}, bf16[1152,128]{1,0:T(8,128)(2,1)S(1)}, u32[]{:S(2)}, u32[]{:S(2)}) %collective-permute-start.22) | collective-permute-done | bytes 294944 | tf_op jit(solution)/shard_map/ppermute | solution.py:62
  186.0 8.7 %fusion.9 = (bf16[1792,512]{1,0:T(8,128)(2,1)S(1)}, bf16[1792,512]{1,0:T(8,128)(2,1)S(1)}) fusion(f32[1792,512]{1,0:T(8,128)} %copy-done.113, f32[1792,512]{1,0:T(8,128)} %get-tuple-element.193, bf16[1152,128]{1,0:T(8,128)(2,1)S(1)} %collective-permute-done.23, bf16[1152,128]{1,0:T(8,128)(2,1)S(1)} %collective-permute-done.22, ...), kind=kOutput, calls=%fused_computation.20 | convolution fusion | flops 2140667904 | bytes 16318464 | tf_op jit(solution)/shard_map/dot_general | solution.py:78
  207.7 3.3 collective-permute-start.53
  222.8 7.6 %collective-permute-done.28 = bf16[1152,128]{1,0:T(8,128)(2,1)S(1)} collective-permute-done((bf16[1152,128]{1,0:T(8,128)(2,1)S(1)}, bf16[1152,128]{1,0:T(8,128)(2,1)S(1)}, u32[]{:S(2)}, u32[]{:S(2)}) %collective-permute-start.28) | collective-permute-done | bytes 294944 | tf_op jit(solution)/shard_map/ppermute | solution.py:62
  240.6 5.2 %collective-permute-done.30 = bf16[512,512]{1,0:T(8,128)(2,1)S(1)} collective-permute-done((bf16[512,512]{1,0:T(8,128)(2,1)}, bf16[512,512]{1,0:T(8,128)(2,1)S(1)}, u32[]{:S(2)}, u32[]{:S(2)}) %collective-permute-start.30) | collective-permute-done | bytes 524320 | tf_op jit(solution)/shard_map/ppermute | solution.py:36
  249.6 4.2 multiply_reduce_fusion
  253.9 3.5 collective-permute-start.89
  257.4 4.0 convolution_convert_fusion
  284.9 4.0 collective-permute-done.35
  290.2 4.1 collective-permute-done.36
  303.9 8.8 %collective-permute-start.77 = (bf16[2,288,1792]{2,1,0:T(8,128)(2,1)}, bf16[2,288,1792]{2,1,0:T(8,128)(2,1)}, u32[]{:S(2)}, u32[]{:S(2)}) collective-permute-start(bf16[2,288,1792]{2,1,0:T(8,128)(2,1)} %dynamic-slice_bitcast_fusion), channel_id=1, source_target_pairs={{0,8},{8,0},{16,24},{24,16},{32,40},{40,32},{48,56},{56,48},{64,72... | collective-permute-start | bytes 6193160 | tf_op jit(solution)/shard_map/ppermute | solution.py:46
  315.4 4.1 collective-permute-start.38
  330.3 8.6 %collective-permute-done.39 = bf16[2,72,768]{2,1,0:T(8,128)(2,1)S(1)} collective-permute-done((bf16[2,72,768]{2,1,0:T(8,128)(2,1)S(1)}, bf16[2,72,768]{2,1,0:T(8,128)(2,1)S(1)}, u32[]{:S(2)}, u32[]{:S(2)}) %collective-permute-start.39) | collective-permute-done | bytes 221216 | tf_op jit(solution)/shard_map/ppermute | solution.py:51
  340.8 3.1 collective-permute-done.40
  347.2 4.9 %collective-permute-done.41 = bf16[2,72,768]{2,1,0:T(8,128)(2,1)S(1)} collective-permute-done((bf16[2,72,768]{2,1,0:T(8,128)(2,1)S(1)}, bf16[2,72,768]{2,1,0:T(8,128)(2,1)S(1)}, u32[]{:S(2)}, u32[]{:S(2)}) %collective-permute-start.41) | collective-permute-done | bytes 221216 | tf_op jit(solution)/shard_map/ppermute | solution.py:51
  367.1 6.1 %collective-permute-done.46 = bf16[72,768]{1,0:T(8,128)(2,1)S(1)} collective-permute-done((bf16[72,768]{1,0:T(8,128)(2,1)S(1)}, bf16[72,768]{1,0:T(8,128)(2,1)S(1)}, u32[]{:S(2)}, u32[]{:S(2)}) %collective-permute-start.46) | collective-permute-done | bytes 110624 | tf_op jit(solution)/shard_map/ppermute | solution.py:51
  383.6 8.6 %collective-permute-done.48 = bf16[72,768]{1,0:T(8,128)(2,1)S(1)} collective-permute-done((bf16[72,768]{1,0:T(8,128)(2,1)S(1)}, bf16[72,768]{1,0:T(8,128)(2,1)S(1)}, u32[]{:S(2)}, u32[]{:S(2)}) %collective-permute-start.48) | collective-permute-done | bytes 110624 | tf_op jit(solution)/shard_map/ppermute | solution.py:51
  394.1 9.3 %collective-permute-start.49 = (bf16[288,768]{1,0:T(8,128)(2,1)}, bf16[288,768]{1,0:T(8,128)(2,1)}, u32[]{:S(2)}, u32[]{:S(2)}) collective-permute-start(bf16[288,768]{1,0:T(8,128)(2,1)} %pad_maximum_fusion.23), channel_id=1, source_target_pairs={{0,8},{8,0},{16,24},{24,16},{32,40},{40,32},{48,56},{56,48},{64,72... | collective-permute-start | bytes 1327112 | tf_op jit(solution)/shard_map/ppermute | solution.py:46
  462.2 6.8 %collective-permute-start.64 = (bf16[288,1792]{1,0:T(8,128)(2,1)S(1)}, bf16[288,1792]{1,0:T(8,128)(2,1)S(1)}, u32[]{:S(2)}, u32[]{:S(2)}) collective-permute-start(bf16[288,1792]{1,0:T(8,128)(2,1)S(1)} %pad_maximum_fusion.13), channel_id=1, source_target_pairs={{0,8},{8,0},{16,24},{24,16},{32,40},{40,32},{48,56},{56,48},{64,72... | collective-permute-start | bytes 3096584 | tf_op jit(solution)/shard_map/ppermute | solution.py:46
  (637 shorter events, 255.9 us)
Async XLA Ops:
  2.3 19.2 %collective-permute-start = (bf16[576,128]{1,0:T(8,128)(2,1)}, bf16[576,128]{1,0:T(8,128)(2,1)S(1)}, u32[]{:S(2)}, u32[]{:S(2)}) collective-permute-start(bf16[576,128]{1,0:T(8,128)(2,1)} %get-tuple-element.161), channel_id=1, source_target_pairs={{0,1},{8,9},{1,0},{9,8},{16,17},{24,25},{17,16},{25,24},{32,33},{4... | collective-permute-start | bytes 442376 | tf_op jit(solution)/shard_map/ppermute | solution.py:36
  6.7 14.0 %collective-permute-start.3 = (f32[4,576]{1,0:T(4,128)S(1)}, f32[4,576]{1,0:T(4,128)S(1)}, u32[]{:S(2)}, u32[]{:S(2)}) collective-permute-start(f32[4,576]{1,0:T(4,128)S(1)} %pad_maximum_fusion.33), channel_id=1, source_target_pairs={{0,1},{8,9},{1,0},{9,8},{16,17},{24,25},{17,16},{25,24},{32,33},{4... | collective-permute-start | bytes 27656 | tf_op jit(solution)/shard_map/ppermute | solution.py:36
  27.8 48.4 %collective-permute-start.11 = (bf16[288,5376]{1,0:T(8,128)(2,1)}, bf16[288,5376]{1,0:T(8,128)(2,1)}, u32[]{:S(2)}, u32[]{:S(2)}) collective-permute-start(bf16[288,5376]{1,0:T(8,128)(2,1)} %constant_dynamic-slice_fusion.14), channel_id=1, source_target_pairs={{0,17},{8,9},{1,0},{9,24},{16,1},{24,25},{17,16},{25,8},{32,49},{4... | collective-permute-start | bytes 9289736 | tf_op jit(solution)/shard_map/ppermute | solution.py:36
  38.4 15.3 %collective-permute-start.5 = (bf16[1152,128]{1,0:T(8,128)(2,1)}, bf16[1152,128]{1,0:T(8,128)(2,1)}, u32[]{:S(2)}, u32[]{:S(2)}) collective-permute-start(bf16[1152,128]{1,0:T(8,128)(2,1)} %fusion.57), channel_id=1, source_target_pairs={{0,6},{2,0},{4,2},{6,4},{1,7},{3,1},{5,3},{7,5},{8,14},{10,8},{12,... | collective-permute-start | bytes 884744 | tf_op jit(solution)/shard_map/ppermute | solution.py:62
  39.6 14.1 %collective-permute-start.4 = (bf16[1152,128]{1,0:T(8,128)(2,1)}, bf16[1152,128]{1,0:T(8,128)(2,1)}, u32[]{:S(2)}, u32[]{:S(2)}) collective-permute-start(bf16[1152,128]{1,0:T(8,128)(2,1)} %fusion.57), channel_id=1, source_target_pairs={{0,2},{2,4},{4,6},{6,0},{1,3},{3,5},{5,7},{7,1},{8,10},{10,12},{12... | collective-permute-start | bytes 884744 | tf_op jit(solution)/shard_map/ppermute | solution.py:62
  57.7 17.6 %collective-permute-start.7 = (bf16[512,512]{1,0:T(8,128)(2,1)S(1)}, bf16[512,512]{1,0:T(8,128)(2,1)S(1)}, u32[]{:S(2)}, u32[]{:S(2)}) collective-permute-start(bf16[512,512]{1,0:T(8,128)(2,1)S(1)} %pad_maximum_fusion.21), channel_id=1, source_target_pairs={{0,1},{8,9},{1,0},{9,8},{16,17},{24,25},{17,16},{25,24},{32,33},{4... | collective-permute-start | bytes 1572872 | tf_op jit(solution)/shard_map/ppermute | solution.py:36
  76.2 27.4 %collective-permute-start.12 = (bf16[288,5376]{1,0:T(8,128)(2,1)}, bf16[288,5376]{1,0:T(8,128)(2,1)S(1)}, u32[]{:S(2)}, u32[]{:S(2)}) collective-permute-start(bf16[288,5376]{1,0:T(8,128)(2,1)} %collective-permute-done.11), channel_id=1, source_target_pairs={{0,8},{8,0},{16,24},{24,16},{32,40},{40,32},{48,56},{56,48},{64,72... | collective-permute-start | bytes 9289736 | tf_op jit(solution)/shard_map/ppermute | solution.py:46
  83.9 14.7 %collective-permute-start.8 = (bf16[1152,128]{1,0:T(8,128)(2,1)S(1)}, bf16[1152,128]{1,0:T(8,128)(2,1)S(1)}, u32[]{:S(2)}, u32[]{:S(2)}) collective-permute-start(bf16[1152,128]{1,0:T(8,128)(2,1)S(1)} %get-tuple-element.102), channel_id=1, source_target_pairs={{0,4},{2,6},{4,0},{6,2},{1,5},{3,7},{5,1},{7,3},{8,12},{10,14},{12... | collective-permute-start | bytes 884744 | tf_op jit(solution)/shard_map/ppermute | solution.py:62
  100.4 44.0 %collective-permute-start.15 = (bf16[1152,128]{1,0:T(8,128)(2,1)S(1)}, bf16[1152,128]{1,0:T(8,128)(2,1)S(1)}, u32[]{:S(2)}, u32[]{:S(2)}) collective-permute-start(bf16[1152,128]{1,0:T(8,128)(2,1)S(1)} %multiply_convert_fusion.3), channel_id=1, source_target_pairs={{0,4},{2,6},{4,0},{6,2},{1,5},{3,7},{5,1},{7,3},{8,12},{10,14},{12... | collective-permute-start | bytes 884744 | tf_op jit(solution)/shard_map/ppermute | solution.py:62
  101.6 42.8 %collective-permute-start.14 = (bf16[1152,128]{1,0:T(8,128)(2,1)S(1)}, bf16[1152,128]{1,0:T(8,128)(2,1)S(1)}, u32[]{:S(2)}, u32[]{:S(2)}) collective-permute-start(bf16[1152,128]{1,0:T(8,128)(2,1)S(1)} %multiply_convert_fusion.3), channel_id=1, source_target_pairs={{0,6},{2,0},{4,2},{6,4},{1,7},{3,1},{5,3},{7,5},{8,14},{10,8},{12,... | collective-permute-start | bytes 884744 | tf_op jit(solution)/shard_map/ppermute | solution.py:62
  101.9 42.5 %collective-permute-start.13 = (bf16[1152,128]{1,0:T(8,128)(2,1)S(1)}, bf16[1152,128]{1,0:T(8,128)(2,1)S(1)}, u32[]{:S(2)}, u32[]{:S(2)}) collective-permute-start(bf16[1152,128]{1,0:T(8,128)(2,1)S(1)} %multiply_convert_fusion.3), channel_id=1, source_target_pairs={{0,2},{2,4},{4,6},{6,0},{1,3},{3,5},{5,7},{7,1},{8,10},{10,12},{12... | collective-permute-start | bytes 884744 | tf_op jit(solution)/shard_map/ppermute | solution.py:62
  156.8 13.8 %collective-permute-start.16 = (bf16[1152,128]{1,0:T(8,128)(2,1)S(1)}, bf16[1152,128]{1,0:T(8,128)(2,1)S(1)}, u32[]{:S(2)}, u32[]{:S(2)}) collective-permute-start(bf16[1152,128]{1,0:T(8,128)(2,1)S(1)} %get-tuple-element.99), channel_id=1, source_target_pairs={{0,4},{2,6},{4,0},{6,2},{1,5},{3,7},{5,1},{7,3},{8,12},{10,14},{12... | collective-permute-start | bytes 884744 | tf_op jit(solution)/shard_map/ppermute | solution.py:62
  171.7 14.3 %collective-permute-start.22 = (bf16[1152,128]{1,0:T(8,128)(2,1)S(1)}, bf16[1152,128]{1,0:T(8,128)(2,1)S(1)}, u32[]{:S(2)}, u32[]{:S(2)}) collective-permute-start(bf16[1152,128]{1,0:T(8,128)(2,1)S(1)} %get-tuple-element.127), channel_id=1, source_target_pairs={{0,6},{2,0},{4,2},{6,4},{1,7},{3,1},{5,3},{7,5},{8,14},{10,8},{12,... | collective-permute-start | bytes 884744 | tf_op jit(solution)/shard_map/ppermute | solution.py:62
  207.7 112.6 %collective-permute-start.53 = (bf16[2,288,1792]{2,1,0:T(8,128)(2,1)}, bf16[2,288,1792]{2,1,0:T(8,128)(2,1)}, u32[]{:S(2)}, u32[]{:S(2)}) collective-permute-start(bf16[2,288,1792]{2,1,0:T(8,128)(2,1)} %dynamic-slice_bitcast_fusion.2), channel_id=1, source_target_pairs={{0,8},{8,0},{16,24},{24,16},{32,40},{40,32},{48,56},{56,48},{64,72... | collective-permute-start | bytes 6193160 | tf_op jit(solution)/shard_map/ppermute | solution.py:46
  236.2 86.8 %collective-permute-start.65 = (bf16[2,288,1792]{2,1,0:T(8,128)(2,1)}, bf16[2,288,1792]{2,1,0:T(8,128)(2,1)}, u32[]{:S(2)}, u32[]{:S(2)}) collective-permute-start(bf16[2,288,1792]{2,1,0:T(8,128)(2,1)} %dynamic-slice_bitcast_fusion.1), channel_id=1, source_target_pairs={{0,8},{8,0},{16,24},{24,16},{32,40},{40,32},{48,56},{56,48},{64,72... | collective-permute-start | bytes 6193160 | tf_op jit(solution)/shard_map/ppermute | solution.py:46
  277.6 26.3 %collective-permute-start.33 = (bf16[1152,128]{1,0:T(8,128)(2,1)}, bf16[1152,128]{1,0:T(8,128)(2,1)S(1)}, u32[]{:S(2)}, u32[]{:S(2)}) collective-permute-start(bf16[1152,128]{1,0:T(8,128)(2,1)} %get-tuple-element.94), channel_id=1, source_target_pairs={{0,2},{2,4},{4,6},{6,0},{1,3},{3,5},{5,7},{7,1},{8,10},{10,12},{12... | collective-permute-start | bytes 884744 | tf_op jit(solution)/shard_map/ppermute | solution.py:62
  278.9 33.8 %collective-permute-start.32 = (bf16[1152,128]{1,0:T(8,128)(2,1)}, bf16[1152,128]{1,0:T(8,128)(2,1)S(1)}, u32[]{:S(2)}, u32[]{:S(2)}) collective-permute-start(bf16[1152,128]{1,0:T(8,128)(2,1)} %get-tuple-element.95), channel_id=1, source_target_pairs={{0,6},{2,0},{4,2},{6,4},{1,7},{3,1},{5,3},{7,5},{8,14},{10,8},{12,... | collective-permute-start | bytes 884744 | tf_op jit(solution)/shard_map/ppermute | solution.py:62
  303.9 23.7 %collective-permute-start.77 = (bf16[2,288,1792]{2,1,0:T(8,128)(2,1)}, bf16[2,288,1792]{2,1,0:T(8,128)(2,1)}, u32[]{:S(2)}, u32[]{:S(2)}) collective-permute-start(bf16[2,288,1792]{2,1,0:T(8,128)(2,1)} %dynamic-slice_bitcast_fusion), channel_id=1, source_target_pairs={{0,8},{8,0},{16,24},{24,16},{32,40},{40,32},{48,56},{56,48},{64,72... | collective-permute-start | bytes 6193160 | tf_op jit(solution)/shard_map/ppermute | solution.py:46
  322.6 23.6 %collective-permute-start.54 = (bf16[2,72,1792]{2,1,0:T(8,128)(2,1)S(1)}, bf16[2,72,1792]{2,1,0:T(8,128)(2,1)S(1)}, u32[]{:S(2)}, u32[]{:S(2)}) collective-permute-start(bf16[2,72,1792]{2,1,0:T(8,128)(2,1)S(1)} %dynamic-slice_bitcast_fusion.6), channel_id=1, source_target_pairs={{0,32},{8,104},{16,48},{24,120},{32,64},{40,8},{48,80},{56,24},{64... | collective-permute-start | bytes 1548296 | tf_op jit(solution)/shard_map/ppermute | solution.py:51
  325.4 31.1 %collective-permute-start.66 = (bf16[2,72,1792]{2,1,0:T(8,128)(2,1)S(1)}, bf16[2,72,1792]{2,1,0:T(8,128)(2,1)}, u32[]{:S(2)}, u32[]{:S(2)}) collective-permute-start(bf16[2,72,1792]{2,1,0:T(8,128)(2,1)S(1)} %dynamic-slice_bitcast_fusion.5), channel_id=1, source_target_pairs={{0,32},{8,104},{16,48},{24,120},{32,64},{40,8},{48,80},{56,24},{64... | collective-permute-start | bytes 1548296 | tf_op jit(solution)/shard_map/ppermute | solution.py:51
  340.2 21.6 %collective-permute-start.78 = (bf16[2,72,1792]{2,1,0:T(8,128)(2,1)S(1)}, bf16[2,72,1792]{2,1,0:T(8,128)(2,1)}, u32[]{:S(2)}, u32[]{:S(2)}) collective-permute-start(bf16[2,72,1792]{2,1,0:T(8,128)(2,1)S(1)} %dynamic-slice_bitcast_fusion.4), channel_id=1, source_target_pairs={{0,32},{8,104},{16,48},{24,120},{32,64},{40,8},{48,80},{56,24},{64... | collective-permute-start | bytes 1548296 | tf_op jit(solution)/shard_map/ppermute | solution.py:51
  347.2 28.8 %collective-permute-start.55 = (bf16[2,72,1792]{2,1,0:T(8,128)(2,1)}, bf16[2,72,1792]{2,1,0:T(8,128)(2,1)}, u32[]{:S(2)}, u32[]{:S(2)}) collective-permute-start(bf16[2,72,1792]{2,1,0:T(8,128)(2,1)} %fusion.43), channel_id=1, source_target_pairs={{0,32},{8,104},{16,48},{24,120},{32,64},{40,8},{48,80},{56,24},{64... | collective-permute-start | bytes 1548296 | tf_op jit(solution)/shard_map/ppermute | solution.py:51
  358.1 19.1 %collective-permute-start.67 = (bf16[2,72,1792]{2,1,0:T(8,128)(2,1)S(1)}, bf16[2,72,1792]{2,1,0:T(8,128)(2,1)S(1)}, u32[]{:S(2)}, u32[]{:S(2)}) collective-permute-start(bf16[2,72,1792]{2,1,0:T(8,128)(2,1)S(1)} %fusion.40), channel_id=1, source_target_pairs={{0,32},{8,104},{16,48},{24,120},{32,64},{40,8},{48,80},{56,24},{64... | collective-permute-start | bytes 1548296 | tf_op jit(solution)/shard_map/ppermute | solution.py:51
  362.9 17.8 %collective-permute-start.79 = (bf16[2,72,1792]{2,1,0:T(8,128)(2,1)S(1)}, bf16[2,72,1792]{2,1,0:T(8,128)(2,1)S(1)}, u32[]{:S(2)}, u32[]{:S(2)}) collective-permute-start(bf16[2,72,1792]{2,1,0:T(8,128)(2,1)S(1)} %fusion.37), channel_id=1, source_target_pairs={{0,32},{8,104},{16,48},{24,120},{32,64},{40,8},{48,80},{56,24},{64... | collective-permute-start | bytes 1548296 | tf_op jit(solution)/shard_map/ppermute | solution.py:51
  377.1 26.2 %collective-permute-start.56 = (bf16[2,72,1792]{2,1,0:T(8,128)(2,1)S(1)}, bf16[2,72,1792]{2,1,0:T(8,128)(2,1)S(1)}, u32[]{:S(2)}, u32[]{:S(2)}) collective-permute-start(bf16[2,72,1792]{2,1,0:T(8,128)(2,1)S(1)} %fusion.42), channel_id=1, source_target_pairs={{0,32},{8,104},{16,48},{24,120},{32,64},{40,8},{48,80},{56,24},{64... | collective-permute-start | bytes 1548296 | tf_op jit(solution)/shard_map/ppermute | solution.py:51
  379.2 29.9 %collective-permute-start.68 = (bf16[2,72,1792]{2,1,0:T(8,128)(2,1)}, bf16[2,72,1792]{2,1,0:T(8,128)(2,1)}, u32[]{:S(2)}, u32[]{:S(2)}) collective-permute-start(bf16[2,72,1792]{2,1,0:T(8,128)(2,1)} %fusion.39), channel_id=1, source_target_pairs={{0,32},{8,104},{16,48},{24,120},{32,64},{40,8},{48,80},{56,24},{64... | collective-permute-start | bytes 1548296 | tf_op jit(solution)/shard_map/ppermute | solution.py:51
  381.7 32.2 %collective-permute-start.80 = (bf16[2,72,1792]{2,1,0:T(8,128)(2,1)}, bf16[2,72,1792]{2,1,0:T(8,128)(2,1)}, u32[]{:S(2)}, u32[]{:S(2)}) collective-permute-start(bf16[2,72,1792]{2,1,0:T(8,128)(2,1)} %fusion.36), channel_id=1, source_target_pairs={{0,32},{8,104},{16,48},{24,120},{32,64},{40,8},{48,80},{56,24},{64... | collective-permute-start | bytes 1548296 | tf_op jit(solution)/shard_map/ppermute | solution.py:51
  394.1 24.7 %collective-permute-start.49 = (bf16[288,768]{1,0:T(8,128)(2,1)}, bf16[288,768]{1,0:T(8,128)(2,1)}, u32[]{:S(2)}, u32[]{:S(2)}) collective-permute-start(bf16[288,768]{1,0:T(8,128)(2,1)} %pad_maximum_fusion.23), channel_id=1, source_target_pairs={{0,8},{8,0},{16,24},{24,16},{32,40},{40,32},{48,56},{56,48},{64,72... | collective-permute-start | bytes 1327112 | tf_op jit(solution)/shard_map/ppermute | solution.py:46
  405.3 17.2 %collective-permute-start.59 = (bf16[72,896]{1,0:T(8,128)(2,1)}, bf16[72,896]{1,0:T(8,128)(2,1)}, u32[]{:S(2)}, u32[]{:S(2)}) collective-permute-start(bf16[72,896]{1,0:T(8,128)(2,1)} %bitcast.331), channel_id=1, source_target_pairs={{0,16},{8,24},{1,17},{9,25},{16,0},{24,8},{17,1},{25,9},{32,48},{4... | collective-permute-start | bytes 387080 | tf_op jit(solution)/shard_map/ppermute | solution.py:36
  407.2 15.4 %collective-permute-start.58 = (bf16[72,896]{1,0:T(8,128)(2,1)}, bf16[72,896]{1,0:T(8,128)(2,1)}, u32[]{:S(2)}, u32[]{:S(2)}) collective-permute-start(bf16[72,896]{1,0:T(8,128)(2,1)} %bitcast.332), channel_id=1, source_target_pairs={{0,17},{8,25},{1,16},{9,24},{16,1},{24,9},{17,0},{25,8},{32,49},{4... | collective-permute-start | bytes 387080 | tf_op jit(solution)/shard_map/ppermute | solution.py:36
  409.1 16.1 %collective-permute-start.57 = (bf16[72,896]{1,0:T(8,128)(2,1)}, bf16[72,896]{1,0:T(8,128)(2,1)}, u32[]{:S(2)}, u32[]{:S(2)}) collective-permute-start(bf16[72,896]{1,0:T(8,128)(2,1)} %bitcast.333), channel_id=1, source_target_pairs={{0,1},{8,9},{1,0},{9,8},{16,17},{24,25},{17,16},{25,24},{32,33},{4... | collective-permute-start | bytes 387080 | tf_op jit(solution)/shard_map/ppermute | solution.py:36
  413.8 13.7 %collective-permute-start.71 = (bf16[72,896]{1,0:T(8,128)(2,1)}, bf16[72,896]{1,0:T(8,128)(2,1)}, u32[]{:S(2)}, u32[]{:S(2)}) collective-permute-start(bf16[72,896]{1,0:T(8,128)(2,1)} %bitcast.328), channel_id=1, source_target_pairs={{0,16},{8,24},{1,17},{9,25},{16,0},{24,8},{17,1},{25,9},{32,48},{4... | collective-permute-start | bytes 387080 | tf_op jit(solution)/shard_map/ppermute | solution.py:36
  (184 other events, 1383.0 us)
